TPU v7x, 128 devices: a whole 4x4x4 slice. The times are simulated.
128 devices in a mesh: wide: 64 (over z, y_hi, x, core), narrow: 2 (over y_lo).
Axes of the slice: x: 4, y: 4 (y_hi: 2, y_lo: 2; y = y_hi * 2 + y_lo), z: 4, core: 2. Of those that a mesh axis runs over, the one named last changes fastest.
Arguments:
- tokens: bfloat16 [128, 256, 512], P('wide', 'narrow'), may hold values from -6 to 6
- captions: bfloat16 [128, 128, 768], P('wide'), may hold values from -6 to 6
- caption_len: int32 [128], P('wide'), may hold values from 8 to 128, as said below
- timestep: int32 [128], P('wide'), may hold values from 0 to 999
- time_table: float32 [1000, 512], replicated, may hold values from -6 to 6
- cotangent: bfloat16 [128, 256, 512], P('wide', 'narrow'), may hold values from -6 to 6
- w_ada: float32 [512, 3072], P('wide'), may hold values from -0.25 to 0.25
- w_qkv: float32 [512, 1536], P('wide'), may hold values from -0.375 to 0.375
- w_out: float32 [512, 512], P('wide'), may hold values from -0.75 to 0.75
- w_cq: float32 [512, 512], P('wide'), may hold values from -0.375 to 0.375
- w_ckv: float32 [768, 1024], P('wide'), may hold values from -0.3125 to 0.3125
- w_cout: float32 [512, 512], P('wide'), may hold values from -0.5 to 0.5
- w_up: float32 [512, 2048], P('wide'), may hold values from -0.25 to 0.25
- w_down: float32 [2048, 512], P('wide'), may hold values from -0.125 to 0.125
- m_ada: float32 [512, 3072], P('wide'), may hold values from -512 to 512
- m_qkv: float32 [512, 1536], P('wide'), may hold values from -1024 to 1024
- m_out: float32 [512, 512], P('wide'), may hold values from -512 to 512
- m_cq: float32 [512, 512], P('wide'), may hold values from -512 to 512
- m_ckv: float32 [768, 1024], P('wide'), may hold values from -512 to 512
- m_cout: float32 [512, 512], P('wide'), may hold values from -512 to 512
- m_up: float32 [512, 2048], P('wide'), may hold values from -512 to 512
- m_down: float32 [2048, 512], P('wide'), may hold values from -512 to 512
Outputs:
- output: bfloat16 [128, 256, 512], P('wide', 'narrow')
- grad_tokens: float32 [128, 256, 512], P('wide', 'narrow')
- grad_captions: float32 [128, 128, 768], P('wide', 'narrow')
- new_m_ada: float32 [512, 3072], P('wide')
- new_m_qkv: float32 [512, 1536], P('wide')
- new_m_out: float32 [512, 512], P('wide')
- new_m_cq: float32 [512, 512], P('wide')
- new_m_ckv: float32 [768, 1024], P('wide')
- new_m_cout: float32 [512, 512], P('wide')
- new_m_up: float32 [512, 2048], P('wide')
- new_m_down: float32 [2048, 512], P('wide')
- new_w_ada: float32 [512, 3072], P('wide')
- new_w_qkv: float32 [512, 1536], P('wide')
- new_w_out: float32 [512, 512], P('wide')
- new_w_cq: float32 [512, 512], P('wide')
- new_w_ckv: float32 [768, 1024], P('wide')
- new_w_cout: float32 [512, 512], P('wide')
- new_w_up: float32 [512, 2048], P('wide')
- new_w_down: float32 [2048, 512], P('wide')
Inputs may be any that keep to these rules, and one draw needn't show every extreme that they name: `caption_len`: each image has at least 8 live caption tokens; in every draw some image has all 128.
All inputs are finite; a program needn't handle non-finite values.
Results may differ from a plain program's by a relative error of at most 0.025.
The roundings to bfloat16 on the way count: a program that leaves them out, or rounds other values in their place, can miss the bound.
Values may be sent and summed in bfloat16 or wider, within the bound.
No kernel may reach another device: no remote copies, remote signals or barrier semaphores. Data moves between devices by JAX's collectives and lax.ppermute only.
A program may use at most 192 MiB of HBM per device.

v0:
```python
import math

import jax
import jax.numpy as jnp
from jax import lax
from jax.sharding import PartitionSpec as P

D = 512
HEADS = 8
HEAD = 64
NEWTON_STEPS = 5


EPSILON = 1e-06
MASKED = -1e30
RATE = 1.0
DECAY = 0.5
COEF_A = 3.4445
COEF_B = -4.775
COEF_C = 2.0315


def spread_2(array, axis, root):
    mine = lax.axis_index(axis) == root
    return lax.psum(jnp.where(mine, array, jnp.zeros_like(array)), axis)


def layer_norm(signal):
    centre = jnp.mean(signal, axis=-1, keepdims=True)
    centred = signal - centre
    spread = jnp.mean(centred * centred, axis=-1, keepdims=True)
    return centred * lax.rsqrt(spread + EPSILON)


def norm_back(signal, upstream):
    unused, pullback = jax.vjp(layer_norm, signal)
    return pullback(upstream)[0]


def matmul(left, right, form):
    return jnp.einsum(form, left, right, preferred_element_type=jnp.float32)


def exact_dot(left, right):
    return jnp.dot(left, right, precision=lax.Precision.HIGHEST, preferred_element_type=jnp.float32)


def split_heads(signal):
    return signal.reshape(signal.shape[0], signal.shape[1], HEADS, HEAD)


def scores_of(queries, keys_in, allowed):
    raw = matmul(split_heads(queries), split_heads(keys_in), "bqhd,bkhd->bhqk") * HEAD ** (-0.5)
    return jnp.where(allowed, raw, MASKED)


def attend(queries, keys_in, values_in, allowed):
    scores = scores_of(queries, keys_in, allowed)
    row_max = jnp.max(scores, axis=-1, keepdims=True)
    raised = jnp.exp(scores - row_max)
    totals = jnp.sum(raised, axis=-1, keepdims=True)
    weights = (raised / totals).astype(jnp.bfloat16)
    mixed = matmul(weights, split_heads(values_in), "bhqk,bkhd->bqhd")
    return (mixed.reshape(queries.shape).astype(jnp.bfloat16), row_max + jnp.log(totals))


def attend_back(queries, keys_in, values_in, allowed, log_total, upstream):
    scores = scores_of(queries, keys_in, allowed)
    probs = jnp.exp(scores - log_total)
    weights = probs.astype(jnp.bfloat16)
    upstream_heads = split_heads(upstream)
    grad_probs = matmul(upstream_heads, split_heads(values_in), "bqhd,bkhd->bhqk")
    grad_values = matmul(weights, upstream_heads, "bhqk,bqhd->bkhd")
    grad_scores = (
        probs * (grad_probs - jnp.sum(probs * grad_probs, axis=-1, keepdims=True))
    ).astype(jnp.bfloat16)
    grad_queries = matmul(grad_scores, split_heads(keys_in), "bhqk,bkhd->bqhd") * HEAD ** (-0.5)
    grad_keys = matmul(grad_scores, split_heads(queries), "bhqk,bqhd->bkhd") * HEAD ** (-0.5)
    return (
        grad_queries.reshape(queries.shape),
        grad_keys.reshape(keys_in.shape),
        grad_values.reshape(keys_in.shape),
    )


def orthogonal(matrix):
    flipped = matrix.shape[0] > matrix.shape[1]
    work = matrix.T if flipped else matrix
    magnitude = jnp.sqrt(jnp.sum(work * work)) + 1e-07
    iterate = work / magnitude
    for turn in range(NEWTON_STEPS):
        square = exact_dot(iterate, iterate.T)
        quartic = exact_dot(square, square)
        poly = COEF_B * square + COEF_C * quartic
        iterate = COEF_A * iterate + exact_dot(poly, iterate)
    result = iterate.T if flipped else iterate
    return result


def nothing_owned(matrix):
    return jnp.zeros(matrix.shape, jnp.float32)


def body(
    tokens,
    captions,
    caption_len,
    timestep,
    time_table,
    cotangent,
    w_ada,
    w_qkv,
    w_out,
    w_cq,
    w_ckv,
    w_cout,
    w_up,
    w_down,
    m_ada,
    m_qkv,
    m_out,
    m_cq,
    m_ckv,
    m_cout,
    m_up,
    m_down,
):
    masters = (w_ada, w_qkv, w_out, w_cq, w_ckv, w_cout, w_up, w_down)
    momenta = (m_ada, m_qkv, m_out, m_cq, m_ckv, m_cout, m_up, m_down)
    gathered = (
        lax.all_gather(w_ada.astype(jnp.bfloat16), "wide", axis=0, tiled=True),
        lax.all_gather(w_qkv.astype(jnp.bfloat16), "wide", axis=0, tiled=True),
        lax.all_gather(w_out.astype(jnp.bfloat16), "wide", axis=0, tiled=True),
        lax.all_gather(w_cq.astype(jnp.bfloat16), "wide", axis=0, tiled=True),
        lax.all_gather(w_ckv.astype(jnp.bfloat16), "wide", axis=0, tiled=True),
        lax.all_gather(w_cout.astype(jnp.bfloat16), "wide", axis=0, tiled=True),
        lax.all_gather(w_up.astype(jnp.bfloat16), "wide", axis=0, tiled=True),
        lax.all_gather(w_down.astype(jnp.bfloat16), "wide", axis=0, tiled=True),
    )
    full_ada, full_qkv, full_out, full_cq, full_ckv, full_cout, full_up, full_down = gathered
    picks = (timestep[:, None] == jnp.arange(time_table.shape[0])[None, :]).astype(jnp.float32)
    embedded = jnp.dot(
        picks, time_table, precision=lax.Precision.HIGHEST, preferred_element_type=jnp.float32
    )
    time_gate = jax.nn.silu(embedded).astype(jnp.bfloat16)
    modulation = jnp.dot(time_gate, full_ada, preferred_element_type=jnp.float32)
    shift_a, scale_a, gate_a, shift_m, scale_m, gate_m = [
        segment[:, None, :] for segment in jnp.split(modulation, 6, axis=1)
    ]
    inputs = tokens.astype(jnp.float32)
    normed_a = layer_norm(inputs)
    hidden_a = (normed_a * (1.0 + scale_a) + shift_a).astype(jnp.bfloat16)
    projected = matmul(hidden_a, full_qkv, "bsd,de->bse").astype(jnp.bfloat16)
    queries = projected[..., :D]
    keys_own = projected[..., D : 2 * D]
    values_own = projected[..., 2 * D :]
    keys_all, values_all = (
        lax.all_gather(keys_own, "narrow", axis=1, tiled=True),
        lax.all_gather(values_own, "narrow", axis=1, tiled=True),
    )
    mixed_a, total_a = attend(queries, keys_all, values_all, True)
    branch_a = matmul(mixed_a, full_out, "bsd,de->bse")
    after_a = inputs + gate_a * branch_a
    hidden_c = layer_norm(after_a).astype(jnp.bfloat16)
    cross_q = matmul(hidden_c, full_cq, "bsd,de->bse").astype(jnp.bfloat16)
    cross_kv = matmul(captions, full_ckv, "btd,de->bte").astype(jnp.bfloat16)
    live = (jnp.arange(captions.shape[1])[None, :] < caption_len[:, None])[:, None, None, :]
    mixed_c, total_c = attend(cross_q, cross_kv[..., :D], cross_kv[..., D:], live)
    after_c = after_a + matmul(mixed_c, full_cout, "bsd,de->bse")
    normed_m = layer_norm(after_c)
    hidden_m = (normed_m * (1.0 + scale_m) + shift_m).astype(jnp.bfloat16)
    upward = matmul(hidden_m, full_up, "bsd,df->bsf")
    active = jax.nn.gelu(upward).astype(jnp.bfloat16)
    branch_m = matmul(active, full_down, "bsf,fd->bsd")
    result = after_c + gate_m * branch_m
    grad_out = cotangent.astype(jnp.float32)
    grad_branch_m = (gate_m * grad_out).astype(jnp.bfloat16)
    grad_gate_m = jnp.sum(branch_m * grad_out, axis=1)
    grad_active = matmul(grad_branch_m, full_down, "bsd,fd->bsf")
    unused, gelu_pull = jax.vjp(jax.nn.gelu, upward)
    grad_up = gelu_pull(grad_active)[0].astype(jnp.bfloat16)
    grad_hidden_m = matmul(grad_up, full_up, "bsf,df->bsd")
    grad_shift_m = jnp.sum(grad_hidden_m, axis=1)
    grad_scale_m = jnp.sum(grad_hidden_m * normed_m, axis=1)
    grad_c = grad_out + norm_back(after_c, grad_hidden_m * (1.0 + scale_m))
    grad_branch_c = grad_c.astype(jnp.bfloat16)
    grad_mixed_c = matmul(grad_branch_c, full_cout, "bsd,ed->bse").astype(jnp.bfloat16)
    grad_cq_part, grad_ck_part, grad_cv_part = attend_back(
        cross_q, cross_kv[..., :D], cross_kv[..., D:], live, total_c, grad_mixed_c
    )
    grad_cross_q = grad_cq_part.astype(jnp.bfloat16)
    summed_ck, summed_cv = (
        lax.psum_scatter(
            grad_ck_part.astype(jnp.bfloat16), "narrow", scatter_dimension=1, tiled=True
        ).astype(jnp.float32),
        lax.psum_scatter(
            grad_cv_part.astype(jnp.bfloat16), "narrow", scatter_dimension=1, tiled=True
        ).astype(jnp.float32),
    )
    grad_cross_kv = jnp.concatenate([summed_ck, summed_cv], axis=-1).astype(jnp.bfloat16)
    half_rows = summed_ck.shape[1]
    own_words = lax.dynamic_slice_in_dim(
        captions, lax.axis_index("narrow") * half_rows, half_rows, 1
    )
    grad_captions = matmul(grad_cross_kv, full_ckv, "bte,de->btd")
    grad_a = grad_c + norm_back(after_a, matmul(grad_cross_q, full_cq, "bse,de->bsd"))
    grad_branch_a = (gate_a * grad_a).astype(jnp.bfloat16)
    grad_gate_a = jnp.sum(branch_a * grad_a, axis=1)
    grad_mixed_a = matmul(grad_branch_a, full_out, "bse,de->bsd").astype(jnp.bfloat16)
    keys_back, values_back = (keys_all, values_all)
    grad_q_part, grad_k_part, grad_v_part = attend_back(
        queries, keys_back, values_back, True, total_a, grad_mixed_a
    )
    summed_k, summed_v = (
        lax.psum_scatter(
            grad_k_part.astype(jnp.bfloat16), "narrow", scatter_dimension=1, tiled=True
        ).astype(jnp.float32),
        lax.psum_scatter(
            grad_v_part.astype(jnp.bfloat16), "narrow", scatter_dimension=1, tiled=True
        ).astype(jnp.float32),
    )
    grad_projected = jnp.concatenate([grad_q_part, summed_k, summed_v], axis=-1).astype(
        jnp.bfloat16
    )
    grad_hidden_a = matmul(grad_projected, full_qkv, "bse,de->bsd")
    grad_shift_a = jnp.sum(grad_hidden_a, axis=1)
    grad_scale_a = jnp.sum(grad_hidden_a * normed_a, axis=1)
    grad_tokens = grad_a + norm_back(inputs, grad_hidden_a * (1.0 + scale_a))
    grad_modulation = jnp.concatenate(
        [grad_shift_a, grad_scale_a, grad_gate_a, grad_shift_m, grad_scale_m, grad_gate_m], axis=-1
    )
    part_ada = jnp.einsum("bd,be->de", time_gate.astype(jnp.float32), grad_modulation)
    part_qkv = matmul(hidden_a, grad_projected, "bsd,bse->de")
    part_out = matmul(mixed_a, grad_branch_a, "bsd,bse->de")
    part_cq = matmul(hidden_c, grad_cross_q, "bsd,bse->de")
    part_ckv = matmul(own_words, grad_cross_kv, "btd,bte->de")
    part_cout = matmul(mixed_c, grad_branch_c, "bsd,bse->de")
    part_up = matmul(hidden_m, grad_up, "bsd,bsf->df")
    part_down = matmul(active, grad_branch_m, "bsf,bsd->fd")
    coarse = (
        lax.psum_scatter(part_ada, "wide", scatter_dimension=0, tiled=True),
        lax.psum_scatter(part_qkv, "wide", scatter_dimension=0, tiled=True),
        lax.psum_scatter(part_out, "wide", scatter_dimension=0, tiled=True),
        lax.psum_scatter(part_cq, "wide", scatter_dimension=0, tiled=True),
        lax.psum_scatter(part_ckv, "wide", scatter_dimension=0, tiled=True),
        lax.psum_scatter(part_cout, "wide", scatter_dimension=0, tiled=True),
        lax.psum_scatter(part_up, "wide", scatter_dimension=0, tiled=True),
        lax.psum_scatter(part_down, "wide", scatter_dimension=0, tiled=True),
    )
    reduced = lax.psum(
        (coarse[0], coarse[1], coarse[2], coarse[3], coarse[4], coarse[5], coarse[6], coarse[7]),
        "narrow",
    )
    fresh = [DECAY * moment + grad for moment, grad in zip(momenta, reduced)]
    whole = (
        lax.all_gather(fresh[0], "wide", axis=0, tiled=True),
        lax.all_gather(fresh[1], "wide", axis=0, tiled=True),
        lax.all_gather(fresh[2], "wide", axis=0, tiled=True),
        lax.all_gather(fresh[3], "wide", axis=0, tiled=True),
        lax.all_gather(fresh[4], "wide", axis=0, tiled=True),
        lax.all_gather(fresh[5], "wide", axis=0, tiled=True),
        lax.all_gather(fresh[6], "wide", axis=0, tiled=True),
        lax.all_gather(fresh[7], "wide", axis=0, tiled=True),
    )
    position = lax.axis_index("wide")
    stride = lax.axis_size("wide") // 8
    shares = []
    for member in range(8):
        local = lax.cond(position == member * stride, orthogonal, nothing_owned, whole[member])
        spread = spread_2(local.astype(jnp.bfloat16), "wide", member * stride).astype(local.dtype)
        own_rows = masters[member].shape[0]
        shares.append(lax.dynamic_slice_in_dim(spread, position * own_rows, own_rows, 0))
    renewed = []
    for member in range(8):
        rows_all, cols_all = whole[member].shape
        renewed.append(
            masters[member] - RATE * math.sqrt(max(rows_all, cols_all) / rows_all) * shares[member]
        )
    return (
        result.astype(jnp.bfloat16),
        grad_tokens,
        grad_captions,
        fresh[0],
        fresh[1],
        fresh[2],
        fresh[3],
        fresh[4],
        fresh[5],
        fresh[6],
        fresh[7],
        renewed[0],
        renewed[1],
        renewed[2],
        renewed[3],
        renewed[4],
        renewed[5],
        renewed[6],
        renewed[7],
    )


def solution(mesh):
    placed = (
        P("wide", "narrow", None),
        P("wide", None, None),
        P("wide"),
        P("wide"),
        P(),
        P("wide", "narrow", None),
        P("wide", None),
        P("wide", None),
        P("wide", None),
        P("wide", None),
        P("wide", None),
        P("wide", None),
        P("wide", None),
        P("wide", None),
        P("wide", None),
        P("wide", None),
        P("wide", None),
        P("wide", None),
        P("wide", None),
        P("wide", None),
        P("wide", None),
        P("wide", None),
    )
    return jax.shard_map(
        body,
        mesh=mesh,
        in_specs=placed,
        out_specs=(
            P("wide", "narrow", None),
            P("wide", "narrow", None),
            P("wide", "narrow", None),
            P("wide", None),
            P("wide", None),
            P("wide", None),
            P("wide", None),
            P("wide", None),
            P("wide", None),
            P("wide", None),
            P("wide", None),
            P("wide", None),
            P("wide", None),
            P("wide", None),
            P("wide", None),
            P("wide", None),
            P("wide", None),
            P("wide", None),
            P("wide", None),
        ),
        check_vma=False,
    )
```

profile of v0, /device:TPU:1, one launch (start us, length us, event | category | flops | bytes accessed | tf_op | source)
XLA Modules:
  0.0 3882.6 jit_solution(10741300808718856924)
XLA Ops:
  18.1 105.0 %all_gather.82 = bf16[512,512]{1,0:T(8,128)(2,1)} all-gather(bf16[8,512]{1,0:T(8,128)(2,1)S(1)} %convert_element_type.270), channel_id=1, replica_groups=mesh['wide'=64,'narrow'=2] {'wide'}, dimensions={0}, use_global_device_ids=true | all-gather | bytes 532480 | tf_op jit(solution)/shard_map/all_gather | solution.py:133
  123.8 90.0 %all_gather.84 = bf16[512,512]{1,0:T(8,128)(2,1)S(1)} all-gather(bf16[8,512]{1,0:T(8,128)(2,1)S(1)} %convert_element_type.274), channel_id=1, replica_groups=mesh['wide'=64,'narrow'=2] {'wide'}, dimensions={0}, use_global_device_ids=true | all-gather | bytes 532480 | tf_op jit(solution)/shard_map/all_gather | solution.py:134
  215.4 96.6 %all_gather.85 = bf16[512,512]{1,0:T(8,128)(2,1)} all-gather(bf16[8,512]{1,0:T(8,128)(2,1)S(1)} %convert_element_type.280), channel_id=1, replica_groups=mesh['wide'=64,'narrow'=2] {'wide'}, dimensions={0}, use_global_device_ids=true | all-gather | bytes 532480 | tf_op jit(solution)/shard_map/all_gather | solution.py:136
  313.5 2.5 reshape.225
  323.8 8.4 all_gather.81
  336.0 13.8 all_gather.80
  362.8 3.8 fusion.125
  366.6 4.2 fusion.118
  404.4 2.5 convolution_bitcast_fusion.4
  410.0 16.0 reduce-scatter.16.cloned.1.call-done
  425.9 3.4 convolution_bitcast_fusion
  429.4 3.0 convolution_bitcast_fusion.2
  434.0 3.0 convolution_bitcast_fusion.1
  440.4 3.7 fusion.236
  445.1 16.6 reduce-scatter.20.cloned.1.call-done
  464.2 186.0 %fusion = f32[16,1024]{1,0:T(8,128)S(1)} fusion(f32[768,1024]{1,0:T(8,128)S(1)} %convolution_bitcast_fusion.3), kind=kCustom, calls=%all-reduce-scatter | all-reduce-scatter fusion | flops 1048577 | bytes 3211776
  662.2 8.7 collective-permute-start.14
  670.9 9.1 collective-permute-start.2
  680.0 6.1 collective-permute-start.3
  686.1 2.5 collective-permute-start.4
  690.3 5.5 collective-permute-start.6
  698.0 2.5 collective-permute-start.8
  707.2 84.2 %reduce-scatter.28.cloned.1.call-done = f32[8,512]{1,0:T(8,128)} async-done(((f32[512,512]{1,0:T(8,128)}), f32[8,512]{1,0:T(8,128)}) %reduce-scatter.28.cloned.1.call-update) | async-done | bytes 16400 | tf_op jit(solution)/shard_map/reduce_scatter | solution.py:244
  791.5 330.8 %reduce-scatter.30.cloned.1.call-done = f32[8,512]{1,0:T(8,128)} async-done(((f32[512,512]{1,0:T(8,128)}), f32[8,512]{1,0:T(8,128)}) %reduce-scatter.30.cloned.1.call-update) | async-done | bytes 16400 | tf_op jit(solution)/shard_map/reduce_scatter | solution.py:246
  1122.3 328.6 %reduce-scatter.26.cloned.1.call-done = f32[8,512]{1,0:T(8,128)} async-done(((f32[512,512]{1,0:T(8,128)}), f32[8,512]{1,0:T(8,128)}) %reduce-scatter.26.cloned.1.call-update) | async-done | bytes 16400 | tf_op jit(solution)/shard_map/reduce_scatter | solution.py:243
  1450.8 154.3 %reduce-scatter.24.cloned.1.call-done = f32[8,1536]{1,0:T(8,128)} async-done(((f32[512,1536]{1,0:T(8,128)}), f32[8,1536]{1,0:T(8,128)}) %reduce-scatter.24.cloned.1.call-update) | async-done | bytes 49168 | tf_op jit(solution)/shard_map/reduce_scatter | solution.py:242
  1605.2 332.9 %reduce-scatter.32.cloned.1.call-done = f32[8,2048]{1,0:T(8,128)} async-done(((f32[512,2048]{1,0:T(8,128)}), f32[8,2048]{1,0:T(8,128)}) %reduce-scatter.32.cloned.1.call-update) | async-done | bytes 65552 | tf_op jit(solution)/shard_map/reduce_scatter | solution.py:247
  1938.2 335.3 %reduce-scatter.34.cloned.1.call-done = f32[32,512]{1,0:T(8,128)} async-done(((f32[2048,512]{1,0:T(8,128)}), f32[32,512]{1,0:T(8,128)}) %reduce-scatter.34.cloned.1.call-update) | async-done | bytes 65552 | tf_op jit(solution)/shard_map/reduce_scatter | solution.py:248
  2273.5 162.3 %reduce-scatter.22.cloned.1.call-done = f32[8,3072]{1,0:T(8,128)} async-done(((f32[512,3072]{1,0:T(8,128)}), f32[8,3072]{1,0:T(8,128)}) %reduce-scatter.22.cloned.1.call-update) | async-done | bytes 98320 | tf_op jit(solution)/shard_map/reduce_scatter | solution.py:241
  2435.8 30.9 all-reduce.9.cloned.1.call-done
  2474.0 25.9 all-reduce.11.cloned.1.call-done
  2504.7 66.6 %all-gather.32.cloned.1.call-done = f32[512,512]{1,0:T(8,128)} async-done(((f32[8,512]{1,0:T(8,128)}), f32[512,512]{1,0:T(8,128)}) %all-gather.32.cloned.1.call-update) | async-done | bytes 1048592 | tf_op jit(solution)/shard_map/all_gather | solution.py:261
  2571.3 8.9 conditional.13
  2580.2 57.3 %all-gather.30.cloned.1.call-done = f32[512,512]{1,0:T(8,128)} async-done(((f32[8,512]{1,0:T(8,128)}), f32[512,512]{1,0:T(8,128)}) %all-gather.30.cloned.1.call-update) | async-done | bytes 1048592 | tf_op jit(solution)/shard_map/all_gather | solution.py:259
  2637.4 8.9 conditional.11
  2646.3 57.4 %all-gather.28.cloned.1.call-done = f32[512,512]{1,0:T(8,128)} async-done(((f32[8,512]{1,0:T(8,128)}), f32[512,512]{1,0:T(8,128)}) %all-gather.28.cloned.1.call-update) | async-done | bytes 1048592 | tf_op jit(solution)/shard_map/all_gather | solution.py:258
  2703.8 9.1 conditional.10
  2715.4 61.0 %all-gather.40.cloned.1.call-done = f32[64,12,1024]{2,1,0:T(8,128)} async-done(((f32[1,12,1024]{2,1,0:T(8,128)}), f32[64,12,1024]{2,1,0:T(8,128)}) %all-gather.40.cloned.1.call-update) | async-done | bytes 3145744 | tf_op jit(solution)/shard_map/all_gather | solution.py:260
  2776.4 9.1 conditional.12
  2785.5 61.3 %all-gather.26.cloned.1.call-done = f32[512,1536]{1,0:T(8,128)} async-done(((f32[8,1536]{1,0:T(8,128)}), f32[512,1536]{1,0:T(8,128)}) %all-gather.26.cloned.1.call-update) | async-done | bytes 3145744 | tf_op jit(solution)/shard_map/all_gather | solution.py:257
  2846.8 4.1 conditional.9
  2853.4 65.9 %all-gather.36.cloned.1.call-done = f32[2048,512]{1,0:T(8,128)} async-done(((f32[32,512]{1,0:T(8,128)}), f32[2048,512]{1,0:T(8,128)}) %all-gather.36.cloned.1.call-update) | async-done | bytes 4194320 | tf_op jit(solution)/shard_map/all_gather | solution.py:263
  2919.3 4.8 conditional.15
  2924.1 67.8 %all-gather.34.cloned.1.call-done = f32[512,2048]{1,0:T(8,128)} async-done(((f32[8,2048]{1,0:T(8,128)}), f32[512,2048]{1,0:T(8,128)}) %all-gather.34.cloned.1.call-update) | async-done | bytes 4194320 | tf_op jit(solution)/shard_map/all_gather | solution.py:262
  2991.9 4.3 conditional.14
  2999.2 69.5 %all-gather.24.cloned.1.call-done = f32[512,3072]{1,0:T(8,128)} async-done(((f32[8,3072]{1,0:T(8,128)}), f32[512,3072]{1,0:T(8,128)}) %all-gather.24.cloned.1.call-update) | async-done | bytes 6291472 | tf_op jit(solution)/shard_map/all_gather | solution.py:256
  3072.9 3.0 fusion.235
  3077.7 787.8 %all-reduce.13.cloned.1.call-done = (bf16[512,3072]{1,0:T(8,128)(2,1)}, bf16[512,1536]{1,0:T(8,128)(2,1)}, bf16[512,512]{1,0:T(8,128)(2,1)}, bf16[512,512]{1,0:T...) async-done(((bf16[512,3072]{1,0:T(8,128)(2,1)}, bf16[512,1536]{1,0:T(8,128)(2,1)}, ...) | async-done | bytes 12058640 | tf_op jit(solution)/shard_map/psum | solution.py:25
  (345 shorter events, 143.3 us)
Async XLA Ops:
  7.2 306.3 %all-gather.38.cloned.1.call-start = ((), (), s32[]{:S(2)}) async-start(), calls=%async_computation.33 | async-start | bytes 2129920 | tf_op jit(solution)/shard_map/all_gather | solution.py:135
  8.9 309.5 %all-gather.16.cloned.1.call-start = ((), (), s32[]{:S(2)}) async-start(), calls=%async_computation.11 | async-start | bytes 3194880 | tf_op jit(solution)/shard_map/all_gather | solution.py:131
  10.5 310.4 %all-gather.18.cloned.1.call-start = ((), (), s32[]{:S(2)}) async-start(), calls=%async_computation.12 | async-start | bytes 1597440 | tf_op jit(solution)/shard_map/all_gather | solution.py:132
  12.0 350.9 %all-gather.20.cloned.1.call-start = ((), (), s32[]{:S(2)}) async-start(), calls=%async_computation.13 | async-start | bytes 2129920 | tf_op jit(solution)/shard_map/all_gather | solution.py:137
  13.5 353.1 %all-gather.22.cloned.1.call-start = ((), (), s32[]{:S(2)}) async-start(), calls=%async_computation.14 | async-start | bytes 2129920 | tf_op jit(solution)/shard_map/all_gather | solution.py:138
  15.0 394.9 %reduce-scatter.14.cloned.1.call-start = ((), (), s32[]{:S(2)}) async-start(), calls=%async_computation.15 | async-start | bytes 786432 | tf_op jit(solution)/shard_map/reduce_scatter | solution.py:215
  394.0 31.9 reduce-scatter.16.cloned.1.call-start
  398.9 45.3 %reduce-scatter.18.cloned.1.call-start = ((), (), s32[]{:S(2)}) async-start(), calls=%async_computation.17 | async-start | bytes 393216 | tf_op jit(solution)/shard_map/reduce_scatter | solution.py:193
  401.4 60.3 %reduce-scatter.20.cloned.1.call-start = ((), (), s32[]{:S(2)}) async-start(), calls=%async_computation.18 | async-start | bytes 393216 | tf_op jit(solution)/shard_map/reduce_scatter | solution.py:196
  402.8 388.7 %reduce-scatter.28.cloned.1.call-start = ((), (), s32[]{:S(2)}) async-start(), calls=%async_computation.22 | async-start | bytes 1064960 | tf_op jit(solution)/shard_map/reduce_scatter | solution.py:244
  404.3 717.9 %reduce-scatter.30.cloned.1.call-start = ((), (), s32[]{:S(2)}) async-start(), calls=%async_computation.23 | async-start | bytes 1064960 | tf_op jit(solution)/shard_map/reduce_scatter | solution.py:246
  406.9 1044.0 %reduce-scatter.26.cloned.1.call-start = ((), (), s32[]{:S(2)}) async-start(), calls=%async_computation.21 | async-start | bytes 1064960 | tf_op jit(solution)/shard_map/reduce_scatter | solution.py:243
  409.2 1196.0 %reduce-scatter.24.cloned.1.call-start = ((), (), s32[]{:S(2)}) async-start(), calls=%async_computation.20 | async-start | bytes 3194880 | tf_op jit(solution)/shard_map/reduce_scatter | solution.py:242
  429.4 1508.8 %reduce-scatter.32.cloned.1.call-start = ((), (), s32[]{:S(2)}) async-start(), calls=%async_computation.24 | async-start | bytes 4259840 | tf_op jit(solution)/shard_map/reduce_scatter | solution.py:247
  432.4 1841.0 %reduce-scatter.34.cloned.1.call-start = ((), (), s32[]{:S(2)}) async-start(), calls=%async_computation.25 | async-start | bytes 4259840 | tf_op jit(solution)/shard_map/reduce_scatter | solution.py:248
  437.1 1998.7 %reduce-scatter.22.cloned.1.call-start = ((), (), s32[]{:S(2)}) async-start(), calls=%async_computation.19 | async-start | bytes 6389760 | tf_op jit(solution)/shard_map/reduce_scatter | solution.py:241
  444.1 2022.6 %all-reduce.9.cloned.1.call-start = ((), (), s32[]{:S(2)}) async-start(), calls=%async_computation.35 | async-start | bytes 327680 | tf_op jit(solution)/shard_map/psum | solution.py:250
  464.2 2002.4 %copy-start.68 = (f32[8,512]{1,0:T(8,128)S(1)}, f32[8,512]{1,0:T(8,128)}, u32[]{:S(2)}) copy-start(f32[8,512]{1,0:T(8,128)} %param.57) | copy-start | bytes 49156
  464.2 2006.7 %copy-start.59 = (f32[12,1024]{1,0:T(8,128)S(1)}, f32[12,1024]{1,0:T(8,128)}, u32[]{:S(2)}) copy-start(f32[12,1024]{1,0:T(8,128)} %param.56) | copy-start | bytes 147460
  650.3 1849.6 %copy-start.60 = (f32[32,512]{1,0:T(8,128)S(1)}, f32[32,512]{1,0:T(8,128)}, u32[]{:S(2)}) copy-start(f32[32,512]{1,0:T(8,128)} %param.59) | copy-start | bytes 196612
  650.3 1851.1 %copy-start.61 = (f32[8,2048]{1,0:T(8,128)S(1)}, f32[8,2048]{1,0:T(8,128)}, u32[]{:S(2)}) copy-start(f32[8,2048]{1,0:T(8,128)} %param.58) | copy-start | bytes 196612
  650.3 1852.7 %copy-start.56 = (f32[8,3072]{1,0:T(8,128)S(1)}, f32[8,3072]{1,0:T(8,128)}, u32[]{:S(2)}) copy-start(f32[8,3072]{1,0:T(8,128)} %param.52) | copy-start | bytes 294916
  650.4 7.3 collective-permute-start.15
  651.8 9.1 collective-permute-start
  653.8 8.4 collective-permute-start.1
  655.1 15.8 collective-permute-start.10
  656.4 23.6 collective-permute-start.11
  657.7 28.4 collective-permute-start.12
  660.9 27.8 collective-permute-start.13
  662.2 28.1 collective-permute-start.14
  670.9 24.9 collective-permute-start.2
  680.0 18.0 collective-permute-start.3
  686.1 14.4 collective-permute-start.4
  688.6 15.7 collective-permute-start.5
  690.3 14.1 collective-permute-start.6
  695.8 8.6 collective-permute-start.7
  698.0 6.4 collective-permute-start.8
  700.5 3.9 collective-permute-start.9
  1605.2 894.7 %all-reduce.11.cloned.1.call-start = ((), (), s32[]{:S(2)}) async-start(), calls=%async_computation.36 | async-start | bytes 458752 | tf_op jit(solution)/shard_map/psum | solution.py:250
  2435.8 135.5 %all-gather.32.cloned.1.call-start = ((), (), s32[]{:S(2)}) async-start(), calls=%async_computation.30 | async-start | bytes 1064960 | tf_op jit(solution)/shard_map/all_gather | solution.py:261
  2468.0 169.4 %all-gather.30.cloned.1.call-start = ((), (), s32[]{:S(2)}) async-start(), calls=%async_computation.29 | async-start | bytes 1064960 | tf_op jit(solution)/shard_map/all_gather | solution.py:259
  2469.4 234.3 %all-gather.28.cloned.1.call-start = ((), (), s32[]{:S(2)}) async-start(), calls=%async_computation.28 | async-start | bytes 1064960 | tf_op jit(solution)/shard_map/all_gather | solution.py:258
  2470.9 305.5 %all-gather.40.cloned.1.call-start = ((), (), s32[]{:S(2)}) async-start(), calls=%async_computation.34 | async-start | bytes 4259840 | tf_op jit(solution)/shard_map/all_gather | solution.py:260
  2472.4 374.4 %all-gather.26.cloned.1.call-start = ((), (), s32[]{:S(2)}) async-start(), calls=%async_computation.27 | async-start | bytes 3194880 | tf_op jit(solution)/shard_map/all_gather | solution.py:257
  2473.9 445.4 %all-gather.36.cloned.1.call-start = ((), (), s32[]{:S(2)}) async-start(), calls=%async_computation.32 | async-start | bytes 4259840 | tf_op jit(solution)/shard_map/all_gather | solution.py:263
  2501.4 490.5 %all-gather.34.cloned.1.call-start = ((), (), s32[]{:S(2)}) async-start(), calls=%async_computation.31 | async-start | bytes 4259840 | tf_op jit(solution)/shard_map/all_gather | solution.py:262
  2503.0 565.8 %all-gather.24.cloned.1.call-start = ((), (), s32[]{:S(2)}) async-start(), calls=%async_computation.26 | async-start | bytes 6389760 | tf_op jit(solution)/shard_map/all_gather | solution.py:256
  2504.6 1360.9 %all-reduce.13.cloned.1.call-start = ((), (), s32[]{:S(2)}) async-start(), calls=%async_computation.37 | async-start | bytes 24117248 | tf_op jit(solution)/shard_map/psum | solution.py:25
  (62 other events, 6894.2 us)
Sparse Core Ops, SparseCore 0:
  11.8 71.5 all-gather.37
  87.2 66.5 all-gather.15
  157.7 63.2 all-gather.17
  224.6 64.6 all-gather.19
  292.9 64.5 all-gather.21
  394.1 11.1 reduce-scatter.13
  407.8 18.0 reduce-scatter.15
  428.8 15.1 reduce-scatter.17
  446.5 15.1 reduce-scatter.19
  463.9 327.5 reduce-scatter.27
  793.9 328.2 reduce-scatter.29
  1124.5 326.3 reduce-scatter.25
  1457.0 148.1 reduce-scatter.23
  1607.5 330.5 reduce-scatter.31
  1940.4 333.0 reduce-scatter.33
  2279.6 156.0 reduce-scatter.21
  2438.9 27.7 all-reduce.8
  2469.1 30.7 all-reduce.10
  2503.6 67.5 all-gather.31
  2574.9 62.5 all-gather.29
  2641.2 62.5 all-gather.27
  2707.5 68.8 all-gather.39
  2780.3 66.4 all-gather.25
  2850.4 68.8 all-gather.35
  2923.0 68.8 all-gather.33
  2995.6 73.0 all-gather.23
  3073.0 792.4 all-reduce.12
where the time goes:
time: 3890 us; the launch traced here: 3880 us
  waiting for transfers between devices  3110 us (80%)
  blocking collectives  500 us (13%)
  matrix products  63.1 us (2%)
  starting transfers between devices  51.3 us (1%)
  other arithmetic  49.6 us (1%)
  loops' own time  49 us (1%)
    psum x1, waiting for transfers between devices, spread_2(): return lax.psum(jnp.where(mine, array, jnp.zeros_like(array)), axis)  788 us
    reduce_scatter x1, waiting for transfers between devices, body(): lax.psum_scatter(part_down, 'wide', scatter_dimension=0, tiled=True)  335 us
    reduce_scatter x1, waiting for transfers between devices, body(): lax.psum_scatter(part_up, 'wide', scatter_dimension=0, tiled=True)  333 us
    reduce_scatter x1, waiting for transfers between devices, body(): lax.psum_scatter(part_cout, 'wide', scatter_dimension=0, tiled=True)  331 us
    reduce_scatter x1, waiting for transfers between devices, body(): lax.psum_scatter(part_out, 'wide', scatter_dimension=0, tiled=True)  329 us
    unnamed x1, blocking collectives  186 us
    reduce_scatter x1, waiting for transfers between devices, body(): lax.psum_scatter(part_ada, 'wide', scatter_dimension=0, tiled=True)  162 us
    reduce_scatter x1, waiting for transfers between devices, body(): lax.psum_scatter(part_qkv, 'wide', scatter_dimension=0, tiled=True)  154 us
  transfers between devices with their start and end apart: 43, of which 21 were waited for; matrix products, arithmetic and copies ran while one was open for 8% of the time, Pallas kernels for 0%

commit v1 on v0

v1 whole, which is shorter than its diff:
```python
import math

import jax
import jax.numpy as jnp
from jax import lax
from jax.sharding import Mesh
from jax.sharding import PartitionSpec as P

D = 512
HEADS = 8
HEAD = 64

EPSILON = 1e-06
MASKED = -1e30
RATE = 1.0
DECAY = 0.5
COEF_A = 3.4445
COEF_B = -4.775
COEF_C = 2.0315

BF16 = jnp.bfloat16
F32 = jnp.float32
WIDE = ("z", "yh", "x", "c")
SHAPES = {
    "ada": (512, 3072),
    "qkv": (512, 1536),
    "out": (512, 512),
    "cq": (512, 512),
    "ckv": (768, 1024),
    "cout": (512, 512),
    "up": (512, 2048),
    "down": (2048, 512),
}
NAMES = tuple(SHAPES)
REDUCED = ("qkv", "out", "cq", "ckv", "cout", "up", "down")


def units_of(name):
    rows, cols = SHAPES[name]
    return rows * cols // (64 * 512)


def to_units(shard):
    rows, cols = shard.shape
    blocks = shard.reshape(rows, cols // 512, 512).transpose(1, 0, 2)
    return blocks.reshape(rows * cols // 512, 512)


def from_units(stacked, rows, cols):
    count = stacked.shape[0]
    blocks = stacked.reshape(count, cols // 512, rows, 512).transpose(0, 2, 1, 3)
    return blocks.reshape(count * rows, cols)


def swap(value, axis):
    return lax.ppermute(value, axis, [(0, 1), (1, 0)])


def ordered_pair(own, other, axis, dim):
    first = lax.axis_index(axis) == 0
    return jnp.stack([jnp.where(first, own, other), jnp.where(first, other, own)], axis=dim)


def spread_to(value, axes, count):
    return lax.all_to_all(
        jnp.broadcast_to(value[None], (count,) + value.shape), axes, split_axis=0, concat_axis=0, tiled=True
    )


def layer_norm(signal):
    centre = jnp.mean(signal, axis=-1, keepdims=True)
    centred = signal - centre
    spread = jnp.mean(centred * centred, axis=-1, keepdims=True)
    return centred * lax.rsqrt(spread + EPSILON)


def norm_back(signal, upstream):
    unused, pullback = jax.vjp(layer_norm, signal)
    return pullback(upstream)[0]


def mm(left, right):
    return jnp.dot(left, right, preferred_element_type=F32)


def mm_t(left, right):
    return lax.dot_general(left, right, (((1,), (1,)), ((), ())), preferred_element_type=F32)


def t_mm(left, right):
    return lax.dot_general(left, right, (((0,), (0,)), ((), ())), preferred_element_type=F32)


def heads_of(signal):
    return signal.reshape(signal.shape[0], HEADS, HEAD)


def einsum(form, left, right):
    return jnp.einsum(form, left, right, preferred_element_type=F32)


def attend(queries, keys, values, allowed):
    scores = einsum("qhd,khd->hqk", heads_of(queries), heads_of(keys)) * HEAD ** (-0.5)
    if allowed is not None:
        scores = jnp.where(allowed, scores, MASKED)
    row_max = jnp.max(scores, axis=-1, keepdims=True)
    raised = jnp.exp(scores - row_max)
    probs = raised / jnp.sum(raised, axis=-1, keepdims=True)
    mixed = einsum("hqk,khd->qhd", probs.astype(BF16), heads_of(values))
    return mixed.reshape(queries.shape).astype(BF16), probs


def attend_back(queries, keys, values, probs, upstream):
    weights = probs.astype(BF16)
    grad_probs = einsum("qhd,khd->hqk", heads_of(upstream), heads_of(values))
    grad_values = einsum("hqk,qhd->khd", weights, heads_of(upstream))
    inner = jnp.sum(probs * grad_probs, axis=-1, keepdims=True)
    grad_scores = (probs * (grad_probs - inner)).astype(BF16)
    grad_queries = einsum("hqk,khd->qhd", grad_scores, heads_of(keys)) * HEAD ** (-0.5)
    grad_keys = einsum("hqk,qhd->khd", grad_scores, heads_of(queries)) * HEAD ** (-0.5)
    return (
        grad_queries.reshape(queries.shape).astype(BF16),
        grad_keys.reshape(keys.shape).astype(BF16),
        grad_values.reshape(keys.shape).astype(BF16),
    )


def low_dot(left, right):
    return jnp.dot(left.astype(BF16), right.astype(BF16), preferred_element_type=F32)


def high_dot(left, right):
    return jnp.dot(left, right, precision=lax.Precision.HIGH, preferred_element_type=F32)


def orthogonal_rows(matrix, pick):
    magnitude = jnp.sqrt(jnp.sum(matrix * matrix)) + 1e-07
    iterate = matrix / magnitude
    for turn in range(5):
        dot = low_dot if turn < 3 else high_dot
        square = dot(iterate, iterate.T)
        poly = COEF_B * square + COEF_C * dot(square, square)
        if turn < 4:
            iterate = COEF_A * iterate + dot(poly, iterate)
    return pick(poly, iterate)


def body(
    tokens,
    captions,
    caption_len,
    timestep,
    time_table,
    cotangent,
    *weights,
):
    masters = dict(zip(NAMES, weights[:8]))
    momenta = dict(zip(NAMES, weights[8:]))
    half = lax.axis_index("yl")
    core = lax.axis_index("c")
    low = {name: to_units(masters[name].astype(BF16)) for name in NAMES}

    def one_image(pair):
        return lax.dynamic_index_in_dim(pair, half, 0, keepdims=False)

    def other_image(pair):
        return lax.dynamic_index_in_dim(pair, 1 - half, 0, keepdims=False)

    both = jnp.stack([tokens, cotangent], axis=1)
    arrived = swap(other_image(both), "yl")
    whole = ordered_pair(one_image(both), arrived, "yl", 1).reshape(2, 256, D)
    words = one_image(captions)
    length = lax.dynamic_index_in_dim(caption_len, half, 0, keepdims=False)
    step = lax.dynamic_index_in_dim(timestep, half, 0, keepdims=False)
    embedded = lax.dynamic_slice_in_dim(time_table, step, 1, 0)
    time_gate = jax.nn.silu(embedded).astype(BF16)

    ada = low["ada"].reshape(6, 8, 512)
    early = jnp.concatenate([low["qkv"], ada[0], ada[1]], axis=0)
    middle = jnp.concatenate([low["out"], low["cq"], low["ckv"], low["cout"], ada[2]], axis=0)
    late = jnp.concatenate([low["up"], low["down"], ada[3], ada[4], ada[5]], axis=0)
    late_own = lax.all_gather(late, ("z", "yh", "x"), axis=0, tiled=False)
    early_own = spread_to(early, ("z", "yh", "x"), 32)
    early_all = ordered_pair(early_own, swap(early_own, "c"), "c", 1).reshape(64, -1, 512)
    full_qkv = from_units(early_all[:, :24], 8, 1536)
    full_ada_first = from_units(early_all[:, 24:], 8, 1024)

    modulation_first = mm(time_gate, full_ada_first)
    shift_a, scale_a = modulation_first[:, :D], modulation_first[:, D:]
    inputs = whole[0].astype(F32)
    normed_a = layer_norm(inputs)
    hidden_a = (normed_a * (1.0 + scale_a) + shift_a).astype(BF16)
    projected = mm(hidden_a, full_qkv).astype(BF16)
    queries, keys, values = projected[:, :D], projected[:, D : 2 * D], projected[:, 2 * D :]
    mixed_a, probs_a = attend(queries, keys, values, None)

    middle_own = spread_to(middle, ("z", "yh", "x"), 32)
    middle_all = ordered_pair(middle_own, swap(middle_own, "c"), "c", 1).reshape(64, -1, 512)
    full_out = from_units(middle_all[:, 0:8], 8, 512)
    full_cq = from_units(middle_all[:, 8:16], 8, 512)
    full_ckv = from_units(middle_all[:, 16:40], 12, 1024)
    full_cout = from_units(middle_all[:, 40:48], 8, 512)
    gate_a = mm(time_gate, from_units(middle_all[:, 48:56], 8, 512))

    branch_a = mm(mixed_a, full_out)
    after_a = inputs + gate_a * branch_a
    hidden_c = layer_norm(after_a).astype(BF16)
    cross_q = mm(hidden_c, full_cq).astype(BF16)
    cross_kv = mm(words, full_ckv).astype(BF16)
    live = (jnp.arange(words.shape[0]) < length)[None, None, :]
    cross_k, cross_v = cross_kv[:, :D], cross_kv[:, D:]
    mixed_c, probs_c = attend(cross_q, cross_k, cross_v, live)
    after_c = after_a + mm(mixed_c, full_cout)

    late_all = ordered_pair(late_own, swap(late_own, "c"), "c", 1).reshape(64, -1, 512)
    full_up = from_units(late_all[:, 0:32], 8, 2048)
    full_down = from_units(late_all[:, 32:64], 32, 512)
    modulation_last = mm(time_gate, from_units(late_all[:, 64:88], 8, 1536))
    shift_m, scale_m, gate_m = (
        modulation_last[:, :D],
        modulation_last[:, D : 2 * D],
        modulation_last[:, 2 * D :],
    )
    normed_m = layer_norm(after_c)
    hidden_m = (normed_m * (1.0 + scale_m) + shift_m).astype(BF16)
    upward = mm(hidden_m, full_up)
    active, gelu_pull = jax.vjp(jax.nn.gelu, upward)
    active = active.astype(BF16)
    branch_m = mm(active, full_down)
    result = (after_c + gate_m * branch_m).astype(BF16)

    grad_out = whole[1].astype(F32)
    grad_branch_m = (gate_m * grad_out).astype(BF16)
    grad_gate_m = jnp.sum(branch_m * grad_out, axis=0)
    grad_up = gelu_pull(mm_t(grad_branch_m, full_down))[0].astype(BF16)
    grad_hidden_m = mm_t(grad_up, full_up)
    grad_shift_m = jnp.sum(grad_hidden_m, axis=0)
    grad_scale_m = jnp.sum(grad_hidden_m * normed_m, axis=0)
    grad_c = grad_out + norm_back(after_c, grad_hidden_m * (1.0 + scale_m))
    grad_branch_c = grad_c.astype(BF16)
    grad_mixed_c = mm_t(grad_branch_c, full_cout).astype(BF16)
    grad_cross_q, grad_cross_k, grad_cross_v = attend_back(cross_q, cross_k, cross_v, probs_c, grad_mixed_c)
    grad_cross_kv = jnp.concatenate([grad_cross_k, grad_cross_v], axis=-1)
    grad_words = mm_t(grad_cross_kv, full_ckv)
    grad_a = grad_c + norm_back(after_a, mm_t(grad_cross_q, full_cq))
    grad_branch_a = (gate_a * grad_a).astype(BF16)
    grad_gate_a = jnp.sum(branch_a * grad_a, axis=0)
    grad_mixed_a = mm_t(grad_branch_a, full_out).astype(BF16)
    grad_q, grad_k, grad_v = attend_back(queries, keys, values, probs_a, grad_mixed_a)
    grad_projected = jnp.concatenate([grad_q, grad_k, grad_v], axis=-1)
    grad_hidden_a = mm_t(grad_projected, full_qkv)
    grad_shift_a = jnp.sum(grad_hidden_a, axis=0)
    grad_scale_a = jnp.sum(grad_hidden_a * normed_a, axis=0)
    grad_image = grad_a + norm_back(inputs, grad_hidden_a * (1.0 + scale_a))
    grad_modulation = jnp.stack(
        [grad_shift_a, grad_scale_a, grad_gate_a, grad_shift_m, grad_scale_m, grad_gate_m]
    ).astype(BF16)

    local = {
        "qkv": t_mm(hidden_a, grad_projected),
        "out": t_mm(mixed_a, grad_branch_a),
        "cq": t_mm(hidden_c, grad_cross_q),
        "ckv": t_mm(words, grad_cross_kv),
        "cout": t_mm(mixed_c, grad_branch_c),
        "up": t_mm(hidden_m, grad_up),
        "down": t_mm(active, grad_branch_m),
    }

    def core_part(name, which):
        rows, cols = SHAPES[name]
        blocks = local[name].astype(BF16).reshape(32, 2, rows // 64, cols // 512, 512)
        part = lax.dynamic_index_in_dim(blocks, which, 1, keepdims=False)
        return part.transpose(0, 2, 1, 3).reshape(32, units_of(name), 512)

    kept = jnp.concatenate([core_part(name, core) for name in REDUCED], axis=1)
    sent = jnp.concatenate([core_part(name, 1 - core) for name in REDUCED], axis=1)
    summed = (kept.astype(F32) + swap(sent, "c").astype(F32)).astype(BF16)
    riding = jnp.concatenate([grad_modulation, time_gate], axis=0)
    payload = jnp.concatenate(
        [
            summed.reshape(64, 68, 512),
            jnp.broadcast_to(riding[None], (64, 7, 512)),
        ],
        axis=1,
    )
    received = lax.all_to_all(payload, ("z", "yh", "x", "yl"), split_axis=0, concat_axis=0, tiled=True)
    mine = jnp.sum(received[:, :68].astype(F32), axis=0)
    grads = ordered_pair(mine, swap(mine, "yl"), "yl", 0).reshape(136, 512)
    images_here = received[:, 68:]
    images = jnp.concatenate([images_here, swap(images_here, "c")], axis=0)

    position = lax.axis_index(WIDE)
    gates_here = lax.dynamic_slice_in_dim(images[:, 6].T, position * 8, 8, 0)
    grad_rows = {"ada": mm(gates_here, images[:, :6].reshape(128, 3072))}
    offset = 0
    for name in REDUCED:
        rows, cols = SHAPES[name]
        size = units_of(name)
        grad_rows[name] = from_units(grads[None, offset : offset + size], rows // 64, cols)
        offset += size
    fresh = {name: DECAY * momenta[name] + grad_rows[name] for name in NAMES}

    slots = []
    for name in NAMES:
        block = to_units(fresh[name].astype(BF16))
        slots.append(jnp.pad(block, ((0, 48 - block.shape[0]), (0, 0))))
    owned = lax.all_to_all(jnp.stack(slots), ("z", "yh"), split_axis=0, concat_axis=0, tiled=True)
    owned = spread_to(owned, "x", 4)
    owned = ordered_pair(owned, swap(owned, "c"), "c", 1)
    owned = owned.transpose(2, 0, 1, 3, 4).reshape(64, 48, 512)
    group = lax.axis_index(("x", "c"))

    def branch(name):
        rows, cols = SHAPES[name]
        per = rows // 64

        def work(gathered):
            matrix = from_units(gathered[:, : units_of(name)], per, cols).astype(F32)
            if rows <= cols:

                def pick(poly, iterate):
                    def wanted(value):
                        blocks = value.reshape(8, 8, per, value.shape[-1])
                        return lax.dynamic_index_in_dim(blocks, group, 1, keepdims=False).reshape(8 * per, -1)

                    return COEF_A * wanted(iterate) + high_dot(wanted(poly), iterate)

                update = orthogonal_rows(matrix, pick)
            else:

                def pick(poly, iterate):
                    blocks = iterate.T.reshape(8, 8, per, cols)
                    wanted = lax.dynamic_index_in_dim(blocks, group, 1, keepdims=False).reshape(8 * per, cols)
                    return COEF_A * wanted + high_dot(wanted, poly)

                update = orthogonal_rows(matrix.T, pick)
            update = (RATE * math.sqrt(max(rows, cols) / rows) * update).astype(BF16)
            pieces = update.reshape(8, per, cols // 512, 512).transpose(0, 2, 1, 3)
            pieces = pieces.reshape(8, units_of(name), 512)
            return jnp.pad(pieces, ((0, 0), (0, 48 - pieces.shape[1]), (0, 0)))

        return work

    updates = lax.switch(lax.axis_index(("z", "yh")), [branch(name) for name in NAMES], owned)
    updates = lax.all_to_all(updates, ("z", "yh"), split_axis=0, concat_axis=0, tiled=True)
    renewed = {}
    for index, name in enumerate(NAMES):
        rows, cols = SHAPES[name]
        rows_here = from_units(updates[index : index + 1, : units_of(name)], rows // 64, cols)
        renewed[name] = masters[name] - rows_here.astype(F32)

    def halves(image):
        rows = image.shape[0] // 2
        parts = image.reshape(2, rows, image.shape[1])
        return ordered_pair(one_image(parts), swap(other_image(parts), "yl"), "yl", 0)

    return (
        halves(result),
        halves(grad_image),
        halves(grad_words),
        *[fresh[name] for name in NAMES],
        *[renewed[name] for name in NAMES],
    )


def solution(mesh):
    fine = Mesh(mesh.devices.reshape(4, 2, 4, 2, 2), ("z", "yh", "x", "c", "yl"))
    split = P(WIDE, "yl", None)
    rows = P(WIDE, None)
    placed = (split, P(WIDE, None, None), P(WIDE), P(WIDE), P(), split) + (rows,) * 16
    return jax.shard_map(
        body,
        mesh=fine,
        in_specs=placed,
        out_specs=(split,) * 3 + (rows,) * 16,
        check_vma=False,
    )
```

time: 3890 us -> 527 us (0.14)
  waiting for transfers between devices: 3110 us -> 76.7 us
  blocking collectives: 500 us -> 101 us
  matrix products: 63.1 us -> 131 us
    reduce_scatter x11 -> x0, waiting for transfers between devices: 1760 us -> none  [the longest x1 335 us: body(): lax.psum_scatter(part_down, 'wide', scatter_dimension=0, tiled=True)]
    psum x3 -> x0, waiting for transfers between devices: 845 us -> none  [the longest x1 788 us: spread_2(): return lax.psum(jnp.where(mine, array, jnp.zeros_like(array)), axis)]
    all_gather x13 -> x1, waiting for transfers between devices: 507 us -> 14.3 us  [body(): late_own = lax.all_gather(late, ('z', 'yh', 'x'), axis=0, tiled=False)]
    all_gather x5 -> x0, blocking collectives: 314 us -> none  [the longest x1 105 us: body(): lax.all_gather(w_out.astype(jnp.bfloat16), 'wide', axis=0, tiled=True)]
    unnamed x1 -> x0, blocking collectives: 186 us -> none
    all_to_all x0 -> x3, blocking collectives: none -> 101 us  [the longest x1 68.7 us: body(): lax.all_to_all(payload, ('z', 'yh', 'x', 'yl'), split_axis=0, concat_axis...]
    dot_general x36 -> x47, matrix products: 63.1 us -> 126 us  [the longest x6 39.5 us: low_dot(): jnp.dot(left.astype(BF16), right.astype(BF16), preferred_element_type=F32)]
    unnamed x16 -> x0, starting transfers between devices: 50 us -> none
  transfers between devices with their start and end apart: 43 -> 15, of which waited for: 21 -> 6; matrix products, arithmetic and copies ran while one was open for 8% -> 26% of each run, Pallas kernels for 0% -> 0%
where the time goes in v1:
time: 527 us; the launch traced here: 517 us
  matrix products  131 us (25%)
  blocking collectives  101 us (19%)
  waiting for transfers between devices  76.7 us (15%)
  local copies, waits for them, and re-layouts  58.5 us (11%)
  other arithmetic  51.4 us (10%)
  starting transfers between devices  49.3 us (9%)
  loops' own time  31.5 us (6%)
  between operations  18.1 us (3%)
    all_to_all x1, blocking collectives, body(): lax.all_to_all(payload, ('z', 'yh', 'x', 'yl'), split_axis=0, concat_axis...  68.7 us
    dot_general x6, matrix products, low_dot(): jnp.dot(left.astype(BF16), right.astype(BF16), preferred_element_type=F32)  39.5 us
    ppermute x11, waiting for transfers between devices, swap(): return lax.ppermute(value, axis, [(0, 1), (1, 0)])  36.7 us
    dot_general x6, matrix products, high_dot(): jnp.dot(left, right, precision=lax.Precision.HIGH, preferred_element_type...  33.7 us
    another operation x1, loops' own time, body(): lax.switch(lax.axis_index(('z', 'yh')), [branch(name) for name in NAMES],...  31.5 us
    all_to_all x1, blocking collectives, spread_to(): lax.all_to_all(jnp.broadcast_to(value[None], (count,) + value.shape), axe...  20.3 us
    all_to_all x2, waiting for transfers between devices, spread_to(): lax.all_to_all(jnp.broadcast_to(value[None], (count,) + value.shape), axe...  18.7 us
    unnamed x216, local copies, waits for them, and re-layouts  18.7 us
  transfers between devices with their start and end apart: 15, of which 6 were waited for; matrix products, arithmetic and copies ran while one was open for 26% of the time, Pallas kernels for 0%

profile of v1, /device:TPU:1, one launch (start us, length us, event | category | flops | bytes accessed | tf_op | source)
XLA Modules:
  0.0 517.0 jit_solution(5938079174579777089)
XLA Ops:
  10.3 11.5 %all-to-all-start.1 = ((bf16[32,40,512]{2,1,0:T(8,128)(2,1)}), bf16[32,40,512]{2,1,0:T(8,128)(2,1)}, u32[]{:S(2)}, u32[]{:S(2)}) async-start(bf16[32,40,512]{2,1,0:T(8,128)(2,1)} %broadcast_in_dim.33), calls=%async_computation.1 | async-start | bytes 2621440 | tf_op jit(solution)/shard_map/all_to_all | solution.py:65
  22.7 18.7 %all-to-all-done.1 = bf16[32,40,512]{2,1,0:T(8,128)(2,1)} async-done(((bf16[32,40,512]{2,1,0:T(8,128)(2,1)}), bf16[32,40,512]{2,1,0:T(8,128)(2,1)}, u32[]{:S(2)}, u32[]{:S(2)}) %all-to-all-start.1) | async-done | bytes 1310752 | tf_op jit(solution)/shard_map/all_to_all | solution.py:65
  42.8 5.7 %all-to-all-start = ((bf16[32,56,512]{2,1,0:T(8,128)(2,1)}), bf16[32,56,512]{2,1,0:T(8,128)(2,1)S(1)}, u32[]{:S(2)}, u32[]{:S(2)}) async-start(bf16[32,56,512]{2,1,0:T(8,128)(2,1)} %broadcast_in_dim.32), calls=%async_computation | async-start | bytes 3670016 | tf_op jit(solution)/shard_map/all_to_all | solution.py:65
  55.8 20.5 %collective-permute-done = bf16[2,128,512]{2,1,0:T(8,128)(2,1)S(1)} collective-permute-done((bf16[2,128,512]{2,1,0:T(8,128)(2,1)S(1)}, bf16[2,128,512]{2,1,0:T(8,128)(2,1)S(1)}, u32[]{:S(2)}, u32[]{:S(2)}) %collective-permute-start) | collective-permute-done | bytes 262176 | tf_op jit(solution)/shard_map/ppermute | solution.py:56
  86.4 2.2 fusion.468
  97.2 14.3 %all-gather.3.cloned.1.call-done = bf16[2816,512]{1,0:T(8,128)(2,1)} async-done(((bf16[88,512]{1,0:T(8,128)(2,1)}), bf16[2816,512]{1,0:T(8,128)(2,1)}) %all-gather.3.cloned.1.call-update) | async-done | bytes 2883600 | tf_op jit(solution)/shard_map/all_gather | solution.py:182
  111.5 2.6 collective-permute-start.3
  116.8 2.2 fusion.459
  120.3 2.1 convolution_convert_fusion.12
  125.2 3.0 fusion.469
  128.2 2.4 convolution_convert_fusion.11
  132.4 3.1 select_bitcast_fusion.1
  142.3 2.2 fusion.374
  146.0 2.1 convolution_convert_fusion.10
  157.9 2.9 convolution_convert_fusion.8
  164.5 2.6 convolution_convert_fusion.15
  168.7 2.1 convolution_convert_fusion.7
  170.9 2.1 convolution_convert_fusion.6
  173.4 2.2 convolution_convert_fusion.1
  181.4 3.9 reshape.739
  185.2 2.8 bitcast_dynamic-update-slice_fusion.5
  199.7 7.7 %collective-permute-done.7 = bf16[32,136,512]{2,1,0:T(8,128)(2,1)} collective-permute-done((bf16[32,136,512]{2,1,0:T(8,128)(2,1)}, bf16[32,136,512]{2,1,0:T(8,128)(2,1)}, u32[]{:S(2)}, u32[]{:S(2)}) %collective-permute-start.7) | collective-permute-done | bytes 4456480 | tf_op jit(solution)/shard_map/ppermute | solution.py:56
  207.5 7.0 %add_convert_fusion.3 = bf16[32,136,512]{2,1,0:T(8,128)(2,1)} fusion(bf16[32,136,512]{2,1,0:T(8,128)(2,1)} %collective-permute-done.7, bf16[32,136,512]{2,1,0:T(8,128)(2,1)} %get-tuple-element.185), kind=kLoop, calls=%fused_computation.420 | loop fusion | flops 8912896 | bytes 13369344 | tf_op jit(solution)/shard_map/convert_element_type | solution.py:277
  214.4 7.0 %reshape.748 = bf16[64,68,512]{2,1,0:T(8,128)(2,1)} reshape(bf16[32,136,512]{2,1,0:T(8,128)(2,1)} %add_convert_fusion.3) | data formatting | bytes 8912896 | tf_op jit(solution)/shard_map/reshape | solution.py:281
  221.4 3.3 pad_maximum_fusion.1
  224.8 68.7 %all_to_all.30 = bf16[64,75,512]{2,1,0:T(8,128)(2,1)S(1)} all-to-all(bf16[64,75,512]{2,1,0:T(8,128)(2,1)S(1)} %pad_maximum_fusion.1), channel_id=1, replica_groups=mesh['z'=4,'yh'=2,'x'=4,'c'=2,'yl'=2] {'z','yh','x','yl'}, dimensions={0} | all-to-all | bytes 9830400 | tf_op jit(solution)/shard_map/all_to_all | solution.py:286
  293.5 2.3 copy-done.10
  298.4 2.4 collective-permute-start.8
  308.2 2.1 fusion.471
  310.4 11.8 %all_to_all.31 = bf16[8,48,512]{2,1,0:T(8,128)(2,1)S(1)} all-to-all(bf16[8,48,512]{2,1,0:T(8,128)(2,1)S(1)} %constant_dynamic-update-slice_fusion.10), channel_id=1, replica_groups=mesh['z'=4,'yh'=2,'x'=4,'c'=2,'yl'=2] {'z','yh'}, dimensions={0} | all-to-all | bytes 786432 | tf_op jit(solution)/shard_map/all_to_all | solution.py:307
  322.4 20.3 %all_to_all.32 = bf16[4,8,48,512]{3,2,1,0:T(8,128)(2,1)} all-to-all(bf16[4,8,48,512]{3,2,1,0:T(8,128)(2,1)S(1)} %broadcast_in_dim.43), channel_id=1, replica_groups=mesh['z'=4,'yh'=2,'x'=4,'c'=2,'yl'=2] {'x'}, dimensions={0} | all-to-all | bytes 3145728 | tf_op jit(solution)/shard_map/all_to_all | solution.py:65
  342.7 4.7 collective-permute-start.10
  347.4 2.3 reshape.795
  356.4 8.4 %collective-permute-done.6 = f32[64,768]{1,0:T(8,128)S(1)} collective-permute-done((f32[64,768]{1,0:T(8,128)S(1)}, f32[64,768]{1,0:T(8,128)S(1)}, u32[]{:S(2)}, u32[]{:S(2)}) %collective-permute-start.6) | collective-permute-done | bytes 196640 | tf_op jit(solution)/shard_map/ppermute | solution.py:56
  368.0 112.5 %conditional.1 = (bf16[8,48,512]{2,1,0:T(8,128)(2,1)}) conditional(s32[]{:T(128)} %clamp.3, (bf16[8,4,2,48,512]{4,3,0,1,2:T(8,128)(2,1)S(1)}, s32[]{:T(128)}) %tuple.32, (bf16[8,4,2,48,512]{4,3,0,1,2:T(8,128)(2,1)S(1)}, s32[]{:T(128)}) %tuple.32, (bf16[8,4,2,48,512]{4,3,0,1,2:T(8,128)(2,1)S(1)}, s32[]{:T(128)}) %tuple.32, ...), branch_computations={%region_25.27_spmd, %region_27.29_spmd, %region_29.31_spmd, %regio... | conditional | flops 27213692928 | bytes 222691552 | solution.py:344
  368.1 2.2 fusion
  371.0 3.9 fusion.2
  378.4 7.4 %convolution_add_fusion = f32[512,3072]{1,0:T(8,128)} fusion(f32[512,3072]{1,0:T(8,128)} %bitcast.773, bf16[512,3072]{1,0:T(8,128)(2,1)} %bitcast.798, f32[512,512]{1,0:T(8,128)S(1)} %fusion.472), kind=kOutput, calls=%fused_computation.6 | convolution fusion | flops 1881931776 | bytes 16777216 | tf_op jit(solution)/shard_map/cond/branch_0_fun/dot_general | solution.py:129
  385.8 6.4 %fusion.9 = f32[512,512]{1,0:T(8,128)S(1)} fusion(f32[512,3072]{1,0:T(8,128)} %convolution_add_fusion), kind=kOutput, calls=%fused_computation.16 | convolution fusion | flops 1612185600 | bytes 7340032 | tf_op jit(solution)/shard_map/cond/branch_0_fun/dot_general | solution.py:129
  392.2 8.7 %multiply_add_fusion.2 = f32[512,3072]{1,0:T(8,128)} fusion(f32[512,3072]{1,0:T(8,128)} %convolution_add_fusion, f32[512,512]{1,0:T(8,128)S(1)} %fusion.9), kind=kOutput, calls=%fused_computation.5 | convolution fusion | flops 1885077504 | bytes 13631488 | tf_op jit(solution)/shard_map/cond/branch_0_fun/dot_general | solution.py:129
  400.9 6.4 %fusion.6 = f32[512,512]{1,0:T(8,128)S(1)} fusion(f32[512,3072]{1,0:T(8,128)} %multiply_add_fusion.2), kind=kOutput, calls=%fused_computation.13 | convolution fusion | flops 1612185600 | bytes 7340032 | tf_op jit(solution)/shard_map/cond/branch_0_fun/dot_general | solution.py:129
  407.4 8.7 %multiply_add_fusion.1 = f32[512,3072]{1,0:T(8,128)} fusion(f32[512,3072]{1,0:T(8,128)} %multiply_add_fusion.2, f32[512,512]{1,0:T(8,128)S(1)} %fusion.6), kind=kOutput, calls=%fused_computation.4 | convolution fusion | flops 1885077504 | bytes 13631488 | tf_op jit(solution)/shard_map/cond/branch_0_fun/dot_general | solution.py:129
  416.0 10.4 %fusion.473 = f32[512,512]{1,0:T(8,128)S(1)} fusion(f32[512,3072]{1,0:T(8,128)} %multiply_add_fusion.1), kind=kOutput, calls=%fused_computation.720 | convolution fusion | flops 4831838208 | bytes 7340032 | tf_op jit(solution)/shard_map/cond/branch_0_fun/dot_general | solution.py:133
  427.5 7.9 %multiply_add_fusion = f32[512,3072]{1,0:T(8,128)} fusion(f32[512,3072]{1,0:T(8,128)S(1)} %copy-done.5, f32[512,512]{1,0:T(8,128)S(1)} %fusion.12), kind=kOutput, calls=%fused_computation.3 | convolution fusion | flops 4834983936 | bytes 13631488 | tf_op jit(solution)/shard_map/cond/branch_0_fun/dot_general | solution.py:133
  435.4 10.4 %fusion.474 = f32[512,512]{1,0:T(8,128)S(1)} fusion(f32[512,3072]{1,0:T(8,128)} %multiply_add_fusion), kind=kOutput, calls=%fused_computation.721 | convolution fusion | flops 4831838208 | bytes 7340032 | tf_op jit(solution)/shard_map/cond/branch_0_fun/dot_general | solution.py:133
  447.0 2.9 fusion.4
  480.7 15.4 %all-to-all-start.5 = ((bf16[8,48,512]{2,1,0:T(8,128)(2,1)}), bf16[8,48,512]{2,1,0:T(8,128)(2,1)S(1)}, u32[]{:S(2)}, u32[]{:S(2)}) async-start(bf16[8,48,512]{2,1,0:T(8,128)(2,1)} %get-tuple-element.267), calls=%async_computation.5 | async-start | bytes 786432 | tf_op jit(solution)/shard_map/all_to_all | solution.py:345
  498.0 6.9 %all-to-all-done.5 = bf16[8,48,512]{2,1,0:T(8,128)(2,1)S(1)} async-done(((bf16[8,48,512]{2,1,0:T(8,128)(2,1)}), bf16[8,48,512]{2,1,0:T(8,128)(2,1)S(1)}, u32[]{:S(2)}, u32[]{:S(2)}) %all-to-all-start.5) | async-done | bytes 393248 | tf_op jit(solution)/shard_map/all_to_all | solution.py:345
  (401 shorter events, 110.5 us)
Async XLA Ops:
  7.2 89.6 %copy-start = (bf16[2,128,768]{2,1,0:T(8,128)(2,1)S(1)}, bf16[2,128,768]{2,1,0:T(8,128)(2,1)}, u32[]{:S(2)}) copy-start(bf16[2,128,768]{2,1,0:T(8,128)(2,1)} %param.31) | copy-start | bytes 1179652
  7.2 14.6 %copy-start.74 = (f32[8,512]{1,0:T(8,128)S(1)}, f32[8,512]{1,0:T(8,128)}, u32[]{:S(2)}) copy-start(f32[8,512]{1,0:T(8,128)} %param.38) | copy-start | bytes 49156
  7.2 14.6 %copy-start.57 = (f32[12,1024]{1,0:T(8,128)S(1)}, f32[12,1024]{1,0:T(8,128)}, u32[]{:S(2)}) copy-start(f32[12,1024]{1,0:T(8,128)} %param.40) | copy-start | bytes 147460
  7.2 14.6 %copy-start.59 = (f32[8,2048]{1,0:T(8,128)S(1)}, f32[8,2048]{1,0:T(8,128)}, u32[]{:S(2)}) copy-start(f32[8,2048]{1,0:T(8,128)} %param.42) | copy-start | bytes 196612
  7.2 14.6 %copy-start.76 = (f32[8,512]{1,0:T(8,128)S(1)}, f32[8,512]{1,0:T(8,128)}, u32[]{:S(2)}) copy-start(f32[8,512]{1,0:T(8,128)} %param.39) | copy-start | bytes 49156
  7.3 14.7 %copy-start.63 = (f32[32,512]{1,0:T(8,128)S(1)}, f32[32,512]{1,0:T(8,128)}, u32[]{:S(2)}) copy-start(f32[32,512]{1,0:T(8,128)} %param.43) | copy-start | bytes 196612
  7.3 14.7 %copy-start.78 = (f32[8,512]{1,0:T(8,128)S(1)}, f32[8,512]{1,0:T(8,128)}, u32[]{:S(2)}) copy-start(f32[8,512]{1,0:T(8,128)} %param.41) | copy-start | bytes 49156
  10.3 31.2 %all-to-all-start.1 = ((bf16[32,40,512]{2,1,0:T(8,128)(2,1)}), bf16[32,40,512]{2,1,0:T(8,128)(2,1)}, u32[]{:S(2)}, u32[]{:S(2)}) async-start(bf16[32,40,512]{2,1,0:T(8,128)(2,1)} %broadcast_in_dim.33), calls=%async_computation.1 | async-start | bytes 2621440 | tf_op jit(solution)/shard_map/all_to_all | solution.py:65
  21.7 89.8 %all-gather.3.cloned.1.call-start = ((), (), s32[]{:S(2)}) async-start(), calls=%async_computation.6 | async-start | bytes 2973696 | tf_op jit(solution)/shard_map/all_gather | solution.py:182
  21.8 28.4 %copy-start.52 = (bf16[2,128,512]{2,1,0:T(8,128)(2,1)S(1)}, bf16[2,128,512]{2,1,0:T(8,128)(2,1)}, u32[]{:S(2)}) copy-start(bf16[2,128,512]{2,1,0:T(8,128)(2,1)} %param.30) | copy-start | bytes 786436
  21.8 28.4 %copy-start.53 = (bf16[2,128,512]{2,1,0:T(8,128)(2,1)S(1)}, bf16[2,128,512]{2,1,0:T(8,128)(2,1)}, u32[]{:S(2)}) copy-start(bf16[2,128,512]{2,1,0:T(8,128)(2,1)} %param.35) | copy-start | bytes 786436
  41.5 9.3 %copy-start.110 = (s32[2]{0:T(128)S(1)}, s32[2]{0:T(128)}, u32[]{:S(2)}) copy-start(s32[2]{0:T(128)} %param.33) | copy-start | bytes 28
  41.5 11.2 %copy-start.111 = (s32[2]{0:T(128)S(1)}, s32[2]{0:T(128)}, u32[]{:S(2)}) copy-start(s32[2]{0:T(128)} %param.32) | copy-start | bytes 28
  42.8 34.5 %all-to-all-start = ((bf16[32,56,512]{2,1,0:T(8,128)(2,1)}), bf16[32,56,512]{2,1,0:T(8,128)(2,1)S(1)}, u32[]{:S(2)}, u32[]{:S(2)}) async-start(bf16[32,56,512]{2,1,0:T(8,128)(2,1)} %broadcast_in_dim.32), calls=%async_computation | async-start | bytes 3670016 | tf_op jit(solution)/shard_map/all_to_all | solution.py:65
  48.5 30.8 %collective-permute-start.2 = (bf16[32,40,512]{2,1,0:T(8,128)(2,1)}, bf16[32,40,512]{2,1,0:T(8,128)(2,1)}, u32[]{:S(2)}, u32[]{:S(2)}) collective-permute-start(bf16[32,40,512]{2,1,0:T(8,128)(2,1)} %all-to-all-done.1), channel_id=1, source_target_pairs={{0,2},{2,0},{1,3},{3,1},{4,6},{6,4},{5,7},{7,5},{8,10},{10,8},{9,1... | collective-permute-start | bytes 3932168 | tf_op jit(solution)/shard_map/ppermute | solution.py:56
  50.3 26.0 %collective-permute-start = (bf16[2,128,512]{2,1,0:T(8,128)(2,1)S(1)}, bf16[2,128,512]{2,1,0:T(8,128)(2,1)S(1)}, u32[]{:S(2)}, u32[]{:S(2)}) collective-permute-start(bf16[2,128,512]{2,1,0:T(8,128)(2,1)S(1)} %fusion.398), channel_id=1, source_target_pairs={{0,1},{1,0},{2,3},{3,2},{4,5},{5,4},{6,7},{7,6},{8,9},{9,8},{10,11... | collective-permute-start | bytes 786440 | tf_op jit(solution)/shard_map/ppermute | solution.py:56
  77.3 13.4 %collective-permute-start.1 = (bf16[32,56,512]{2,1,0:T(8,128)(2,1)S(1)}, bf16[32,56,512]{2,1,0:T(8,128)(2,1)}, u32[]{:S(2)}, u32[]{:S(2)}) collective-permute-start(bf16[32,56,512]{2,1,0:T(8,128)(2,1)S(1)} %all-to-all-done), channel_id=1, source_target_pairs={{0,2},{2,0},{1,3},{3,1},{4,6},{6,4},{5,7},{7,5},{8,10},{10,8},{9,1... | collective-permute-start | bytes 5505032 | tf_op jit(solution)/shard_map/ppermute | solution.py:56
  90.6 26.1 %copy-start.40 = (bf16[8,64,256]{2,1,0:T(8,128)(2,1)}, bf16[8,64,256]{2,1,0:T(8,128)(2,1)S(1)}, u32[]{:S(2)}) copy-start(bf16[8,64,256]{2,1,0:T(8,128)(2,1)S(1)} %convolution_convert_fusion.14) | copy-start | bytes 786436
  111.5 20.9 %collective-permute-start.3 = (bf16[32,88,512]{2,1,0:T(8,128)(2,1)}, bf16[32,88,512]{2,1,0:T(8,128)(2,1)}, u32[]{:S(2)}, u32[]{:S(2)}) collective-permute-start(bf16[32,88,512]{2,1,0:T(8,128)(2,1)} %bitcast.832), channel_id=1, source_target_pairs={{0,2},{2,0},{1,3},{3,1},{4,6},{6,4},{5,7},{7,5},{8,10},{10,8},{9,1... | collective-permute-start | bytes 8650760 | tf_op jit(solution)/shard_map/ppermute | solution.py:56
  132.1 10.1 %copy-start.22 = (f32[256,512]{1,0:T(8,128)}, f32[256,512]{1,0:T(8,128)S(1)}, u32[]{:S(2)}) copy-start(f32[256,512]{1,0:T(8,128)S(1)} %get-tuple-element.251) | copy-start | bytes 1572868
  132.1 10.1 %copy-start.96 = (f32[256]{0:T(256)}, f32[256]{0:T(256)S(1)}, u32[]{:S(2)}) copy-start(f32[256]{0:T(256)S(1)} %broadcast_multiply_fusion) | copy-start | bytes 3076
  132.4 9.9 %copy-start.105 = (f32[256]{0:T(256)}, f32[256]{0:T(256)S(1)}, u32[]{:S(2)}) copy-start(f32[256]{0:T(256)S(1)} %fusion.436) | copy-start | bytes 3076
  144.5 7.2 %copy-start.33 = (f32[256,512]{1,0:T(8,128)}, f32[256,512]{1,0:T(8,128)S(1)}, u32[]{:S(2)}) copy-start(f32[256,512]{1,0:T(8,128)S(1)} %get-tuple-element.211) | copy-start | bytes 1572868
  168.7 10.9 %copy-start.38 = (bf16[8,64,128]{2,1,0:T(8,128)(2,1)}, bf16[8,64,128]{2,1,0:T(8,128)(2,1)S(1)}, u32[]{:S(2)}) copy-start(bf16[8,64,128]{2,1,0:T(8,128)(2,1)S(1)} %fusion.369) | copy-start | bytes 393220
  199.6 7.9 %collective-permute-start.7 = (bf16[32,136,512]{2,1,0:T(8,128)(2,1)}, bf16[32,136,512]{2,1,0:T(8,128)(2,1)}, u32[]{:S(2)}, u32[]{:S(2)}) collective-permute-start(bf16[32,136,512]{2,1,0:T(8,128)(2,1)} %get-tuple-element.186), channel_id=1, source_target_pairs={{0,2},{2,0},{1,3},{3,1},{4,6},{6,4},{5,7},{7,5},{8,10},{10,8},{9,1... | collective-permute-start | bytes 13369352 | tf_op jit(solution)/shard_map/ppermute | solution.py:56
  296.6 4.1 collective-permute-start.9
  298.4 5.9 %collective-permute-start.8 = (bf16[64,7,512]{2,1,0:T(8,128)(2,1)S(1)}, bf16[64,7,512]{2,1,0:T(8,128)(2,1)}, u32[]{:S(2)}, u32[]{:S(2)}) collective-permute-start(bf16[64,7,512]{2,1,0:T(8,128)(2,1)S(1)} %slice.246), channel_id=1, source_target_pairs={{0,2},{2,0},{1,3},{3,1},{4,6},{6,4},{5,7},{7,5},{8,10},{10,8},{9,1... | collective-permute-start | bytes 1376264 | tf_op jit(solution)/shard_map/ppermute | solution.py:56
  301.0 7.2 %copy-start.71 = (f32[8,3072]{1,0:T(8,128)S(1)}, f32[8,3072]{1,0:T(8,128)}, u32[]{:S(2)}) copy-start(f32[8,3072]{1,0:T(8,128)} %param.44) | copy-start | bytes 294916
  322.4 27.4 %copy-start.65 = (bf16[256,512]{1,0:T(8,128)(2,1)S(1)}, bf16[256,512]{1,0:T(8,128)(2,1)}, u32[]{:S(2)}) copy-start(bf16[256,512]{1,0:T(8,128)(2,1)} %get-tuple-element.209) | copy-start | bytes 786436
  322.4 28.2 %copy-start.36 = (f32[256,512]{1,0:T(8,128)S(1)}, f32[256,512]{1,0:T(8,128)}, u32[]{:S(2)}) copy-start(f32[256,512]{1,0:T(8,128)} %get-tuple-element.229) | copy-start | bytes 1572868
  322.4 29.6 %copy-start.55 = (bf16[8,64,128]{2,1,0:T(8,128)(2,1)S(1)}, bf16[8,64,128]{2,1,0:T(8,128)(2,1)}, u32[]{:S(2)}) copy-start(bf16[8,64,128]{2,1,0:T(8,128)(2,1)} %convolution_convert_fusion.15) | copy-start | bytes 393220
  342.7 9.7 %copy-start.39 = (bf16[8,64,128]{2,1,0:T(8,128)(2,1)S(1)}, bf16[8,64,128]{2,1,0:T(8,128)(2,1)}, u32[]{:S(2)}) copy-start(bf16[8,64,128]{2,1,0:T(8,128)(2,1)} %copy-done.38) | copy-start | bytes 393220
  342.7 22.9 %collective-permute-start.10 = (bf16[4,8,48,512]{3,2,1,0:T(8,128)(2,1)}, bf16[4,8,48,512]{3,2,1,0:T(8,128)(2,1)}, u32[]{:S(2)}, u32[]{:S(2)}) collective-permute-start(bf16[4,8,48,512]{3,2,1,0:T(8,128)(2,1)} %all_to_all.32), channel_id=1, source_target_pairs={{0,2},{2,0},{1,3},{3,1},{4,6},{6,4},{5,7},{7,5},{8,10},{10,8},{9,1... | collective-permute-start | bytes 4718600 | tf_op jit(solution)/shard_map/ppermute | solution.py:56
  349.8 5.8 %collective-permute-start.4 = (bf16[128,512]{1,0:T(8,128)(2,1)S(1)}, bf16[128,512]{1,0:T(8,128)(2,1)S(1)}, u32[]{:S(2)}, u32[]{:S(2)}) collective-permute-start(bf16[128,512]{1,0:T(8,128)(2,1)S(1)} %dynamic-slice_bitcast_fusion.2), channel_id=1, source_target_pairs={{0,1},{1,0},{2,3},{3,2},{4,5},{5,4},{6,7},{7,6},{8,9},{9,8},{10,11... | collective-permute-start | bytes 393224 | tf_op jit(solution)/shard_map/ppermute | solution.py:56
  351.4 144.7 %collective-permute-start.5 = (f32[128,512]{1,0:T(8,128)}, f32[128,512]{1,0:T(8,128)}, u32[]{:S(2)}, u32[]{:S(2)}) collective-permute-start(f32[128,512]{1,0:T(8,128)} %dynamic-slice_bitcast_fusion), channel_id=1, source_target_pairs={{0,1},{1,0},{2,3},{3,2},{4,5},{5,4},{6,7},{7,6},{8,9},{9,8},{10,11... | collective-permute-start | bytes 786440 | tf_op jit(solution)/shard_map/ppermute | solution.py:56
  354.8 10.1 %collective-permute-start.6 = (f32[64,768]{1,0:T(8,128)S(1)}, f32[64,768]{1,0:T(8,128)S(1)}, u32[]{:S(2)}, u32[]{:S(2)}) collective-permute-start(f32[64,768]{1,0:T(8,128)S(1)} %dynamic-slice_bitcast_fusion.1), channel_id=1, source_target_pairs={{0,1},{1,0},{2,3},{3,2},{4,5},{5,4},{6,7},{7,6},{8,9},{9,8},{10,11... | collective-permute-start | bytes 589832 | tf_op jit(solution)/shard_map/ppermute | solution.py:56
  416.0 11.5 %copy-start.5 = (f32[512,3072]{1,0:T(8,128)S(1)}, f32[512,3072]{1,0:T(8,128)}, u32[]{:S(2)}) copy-start(f32[512,3072]{1,0:T(8,128)} %multiply_add_fusion.1) | copy-start | bytes 18874372 | tf_op jit(solution)/shard_map/cond
  435.4 11.5 %slice-start = ((s8[6291456]{0:T(1024)(128)(4,1)}), s8[2097152]{0:T(1024)(128)(4,1)S(1)}, s32[]{:S(2)}) async-start(s8[6291456]{0:T(1024)(128)(4,1)} %bitcast.768), calls=%async_computation.7 | async-start | bytes 4194304 | tf_op jit(solution)/shard_map/cond
  435.4 11.5 %slice-start.1 = ((s8[6291456]{0:T(1024)(128)(4,1)}), s8[4194304]{0:T(1024)(128)(4,1)S(1)}, s32[]{:S(2)}) async-start(s8[6291456]{0:T(1024)(128)(4,1)} %bitcast.768), calls=%async_computation.8 | async-start | bytes 8388608 | tf_op jit(solution)/shard_map/cond
  480.6 26.0 %copy-start.69 = (f32[8,1536]{1,0:T(8,128)S(1)}, f32[8,1536]{1,0:T(8,128)}, u32[]{:S(2)}) copy-start(f32[8,1536]{1,0:T(8,128)} %param.37) | copy-start | bytes 147460
  480.6 26.7 %copy-start.58 = (f32[12,1024]{1,0:T(8,128)S(1)}, f32[12,1024]{1,0:T(8,128)}, u32[]{:S(2)}) copy-start(f32[12,1024]{1,0:T(8,128)} %param.40) | copy-start | bytes 147460
  480.6 27.4 %copy-start.60 = (f32[8,2048]{1,0:T(8,128)S(1)}, f32[8,2048]{1,0:T(8,128)}, u32[]{:S(2)}) copy-start(f32[8,2048]{1,0:T(8,128)} %param.42) | copy-start | bytes 196612
  480.6 28.0 %copy-start.75 = (f32[8,512]{1,0:T(8,128)S(1)}, f32[8,512]{1,0:T(8,128)}, u32[]{:S(2)}) copy-start(f32[8,512]{1,0:T(8,128)} %param.38) | copy-start | bytes 49156
  480.6 28.0 %copy-start.77 = (f32[8,512]{1,0:T(8,128)S(1)}, f32[8,512]{1,0:T(8,128)}, u32[]{:S(2)}) copy-start(f32[8,512]{1,0:T(8,128)} %param.39) | copy-start | bytes 49156
  480.6 28.0 %copy-start.79 = (f32[8,512]{1,0:T(8,128)S(1)}, f32[8,512]{1,0:T(8,128)}, u32[]{:S(2)}) copy-start(f32[8,512]{1,0:T(8,128)} %param.41) | copy-start | bytes 49156
  480.6 28.6 %copy-start.64 = (f32[32,512]{1,0:T(8,128)S(1)}, f32[32,512]{1,0:T(8,128)}, u32[]{:S(2)}) copy-start(f32[32,512]{1,0:T(8,128)} %param.43) | copy-start | bytes 196612
  480.6 29.2 %copy-start.1 = (bf16[2,128,768]{2,1,0:T(8,128)(2,1)S(1)}, bf16[2,128,768]{2,1,0:T(8,128)(2,1)}, u32[]{:S(2)}) copy-start(bf16[2,128,768]{2,1,0:T(8,128)(2,1)} %param.31) | copy-start | bytes 1179652
  480.7 24.3 %all-to-all-start.5 = ((bf16[8,48,512]{2,1,0:T(8,128)(2,1)}), bf16[8,48,512]{2,1,0:T(8,128)(2,1)S(1)}, u32[]{:S(2)}, u32[]{:S(2)}) async-start(bf16[8,48,512]{2,1,0:T(8,128)(2,1)} %get-tuple-element.267), calls=%async_computation.5 | async-start | bytes 786432 | tf_op jit(solution)/shard_map/all_to_all | solution.py:345
  (68 other events, 239.2 us)
Sparse Core Ops, SparseCore 0:
  26.2 85.2 all-gather.2
